TPU v7x, 256 devices: a whole 4x4x8 slice. The times are simulated.
256 devices in a mesh: slab: 8 (over y, core), lat: 32 (over z, x).
Axes of the slice: x: 4, y: 4, z: 8, core: 2. Of those that a mesh axis runs over, the one named last changes fastest.
Arguments:
- weights: bfloat16 [3072, 16, 128, 128], P(('slab', 'lat')), may hold values from 0.0019989014 to 0.049804688
- angles: float32 [3072, 16, 3, 128], P(('slab', 'lat')), may hold values from 0.2 to 1
- block_list: int32 [3072, 16], P(('slab', 'lat')), may hold values from 0 to 16383, as said below
- observed: float32 [3072, 128], P(('slab', 'lat')), may hold values from -18 to 18
- ray_count: int32 [8, 32], P('slab', 'lat'), may hold values from 384 to 1536, as said below
Outputs:
- solution: float32 [64, 256, 3, 128], P('slab', 'lat')
- residual_ratio: float32 [], replicated
Inputs may be any that keep to these rules, and one draw needn't show every extreme that they name: `block_list`: within the 192 entries of one device's ray tiles, at most 2 name blocks held by any one device (block z * 256 + x is held by slab z // 8, lat x // 8), and on every device some one holder is named exactly 2 times. Each device's live rays are the first ray_count of its rays in tile order; some device has all of them live.
All inputs are finite; a program needn't handle non-finite values.
Results may differ from a plain program's by a relative error of at most 0.004.
Values may be sent and summed in bfloat16 or wider, within the bound.
A program may use at most 64 MiB of HBM per device.

v0:
```python
import jax
import jax.numpy as jnp
from jax import lax
from jax.sharding import PartitionSpec as P

DEPTH_DEV = 8
CROSS_DEV = 8
ITERS = 3


smooth_weight = 0.3
tiny_eps = 1e-06


def extended(block, sides, width):
    for axis, dim in sides:
        count = lax.axis_size(axis)
        forward = [(i, i + 1) for i in range(count - 1)]
        backward = [(target, source) for source, target in forward]
        low = lax.ppermute(
            lax.slice_in_dim(block, block.shape[dim] - width, None, axis=dim), axis, forward
        )
        high = lax.ppermute(lax.slice_in_dim(block, 0, width, axis=dim), axis, backward)
        block = jnp.concatenate([low, block, high], axis=dim)
    return block


def laplace(field_values):
    padded = extended(field_values, (("slab", 0), ("lat", 1)), 1)
    padded = jnp.pad(padded, ((0, 0), (0, 0), (0, 0), (1, 1)))
    centre = padded[1:-1, 1:-1, :, 1:-1]
    beside = padded[2:, 1:-1, :, 1:-1] + padded[:-2, 1:-1, :, 1:-1]
    beside = beside + padded[1:-1, 2:, :, 1:-1] + padded[1:-1, :-2, :, 1:-1]
    beside = beside + padded[1:-1, 1:-1, :, 2:] + padded[1:-1, 1:-1, :, :-2]
    return 6.0 * centre - beside


def total_sum(value):
    return lax.psum(value, ("slab", "lat"))


def slot_ranks(holder, entries):
    entry_order = jnp.arange(entries)
    matches = (holder[None, :] == holder[:, None]) & (entry_order[None, :] < entry_order[:, None])
    return jnp.sum(matches.astype(jnp.int32), axis=1)


def shards(weights, angles, block_list, observed, ray_count):
    tile_count, tile_blocks, ray_width, cell_count = weights.shape
    n_slab = lax.axis_size("slab")
    n_lat = lax.axis_size("lat")
    device_total = n_slab * n_lat
    across = CROSS_DEV * n_lat
    local_blocks = DEPTH_DEV * CROSS_DEV
    entries = tile_count * tile_blocks
    row_width = 3 * cell_count
    capacity = max(2, (2 * entries + device_total - 1) // device_total)
    block_ids = block_list.reshape(entries)
    depth_row = block_ids // across
    lateral = block_ids % across
    owner_slab = depth_row // DEPTH_DEV
    owner_lat = lateral // CROSS_DEV
    inner_block = depth_row % DEPTH_DEV * CROSS_DEV + lateral % CROSS_DEV
    local_shape = (DEPTH_DEV, CROSS_DEV, 3, cell_count)
    holder = owner_slab * n_lat + owner_lat
    slot_at = holder * capacity + slot_ranks(holder, entries)
    slot_total = device_total * capacity
    wanted = jnp.full((slot_total,), -1, jnp.int32).at[slot_at].set(inner_block)
    wanted = wanted.reshape(n_slab, n_lat, capacity)
    requested = lax.all_to_all(
        lax.all_to_all(wanted, "slab", split_axis=0, concat_axis=0, tiled=True),
        "lat",
        split_axis=1,
        concat_axis=1,
        tiled=True,
    ).reshape(slot_total)
    filled = requested >= 0
    picker = (requested[:, None] == jnp.arange(local_blocks)[None, :]).astype(jnp.float32)

    def deliver(partial_value):
        outgoing = jnp.zeros((slot_total, row_width), jnp.float32).at[slot_at].set(partial_value)
        outgoing = outgoing.reshape(n_slab, n_lat, capacity, row_width)
        arrived = lax.all_to_all(
            lax.all_to_all(outgoing, "slab", split_axis=0, concat_axis=0, tiled=True),
            "lat",
            split_axis=1,
            concat_axis=1,
            tiled=True,
        )
        summed = jnp.dot(
            picker.T, arrived.reshape(slot_total, row_width), precision=lax.Precision.HIGHEST
        )
        return summed.reshape(local_shape)

    def adjoint_rays(ray_vec):
        weighted = (angles * ray_vec[:, None, None, :]).astype(jnp.bfloat16)
        partial_value = jnp.einsum(
            "tkac,tkpa->tkpc", weights, weighted, preferred_element_type=jnp.float32
        )
        return deliver(partial_value.reshape(entries, row_width))

    positions = jnp.arange(tile_count)[:, None] * ray_width + jnp.arange(ray_width)[None, :]
    live_rays = (positions < ray_count.reshape(())).astype(jnp.float32)
    ray_vec = observed * live_rays
    first_norm = jnp.sqrt(total_sum(jnp.sum(ray_vec * ray_vec)) + tiny_eps)
    ray_vec = ray_vec / first_norm
    model_vec = adjoint_rays(ray_vec)
    v_norm = jnp.sqrt(total_sum(jnp.sum(model_vec * model_vec)) + tiny_eps)
    model_vec = model_vec / v_norm
    direction = model_vec
    solution = jnp.zeros_like(model_vec)
    cell_vec = jnp.zeros_like(model_vec)
    phi_bar = first_norm
    rho_bar = v_norm
    for iteration in range(ITERS):
        rows_local = model_vec.astype(jnp.bfloat16).reshape(local_blocks, row_width)
        answer = jnp.where(filled[:, None], rows_local[jnp.clip(requested, 0, local_blocks - 1)], 0)
        answer = answer.reshape(n_slab, n_lat, capacity, row_width)
        returned = lax.all_to_all(
            lax.all_to_all(answer, "slab", split_axis=0, concat_axis=0, tiled=True),
            "lat",
            split_axis=1,
            concat_axis=1,
            tiled=True,
        )
        fetched = returned.reshape(slot_total, row_width)[slot_at].reshape(
            tile_count, tile_blocks, 3, cell_count
        )
        product = jnp.einsum(
            "tkac,tkpc->tkpa", weights, fetched, preferred_element_type=jnp.float32
        )
        ray_vec = jnp.sum(product * angles, axis=(1, 2)) * live_rays - v_norm * ray_vec
        cell_vec = smooth_weight * laplace(model_vec) - v_norm * cell_vec
        u_norm = jnp.sqrt(
            total_sum(jnp.sum(ray_vec * ray_vec) + jnp.sum(cell_vec * cell_vec)) + tiny_eps
        )
        ray_vec = ray_vec / u_norm
        cell_vec = cell_vec / u_norm
        model_vec = adjoint_rays(ray_vec) + smooth_weight * laplace(cell_vec) - u_norm * model_vec
        v_norm = jnp.sqrt(total_sum(jnp.sum(model_vec * model_vec)) + tiny_eps)
        model_vec = model_vec / v_norm
        rho_now = jnp.sqrt(rho_bar * rho_bar + u_norm * u_norm)
        cos_term = rho_bar / rho_now
        sin_term = u_norm / rho_now
        theta_now = sin_term * v_norm
        rho_bar = -cos_term * v_norm
        phi_now = cos_term * phi_bar
        phi_bar = sin_term * phi_bar
        solution = solution + phi_now / rho_now * direction
        direction = model_vec - theta_now / rho_now * direction
    return (solution, phi_bar / first_norm)


def solution(mesh):
    placed = (
        P(("slab", "lat"), None, None, None),
        P(("slab", "lat"), None, None, None),
        P(("slab", "lat"), None),
        P(("slab", "lat"), None),
        P("slab", "lat"),
    )
    return jax.shard_map(
        shards,
        mesh=mesh,
        in_specs=placed,
        out_specs=(P("slab", "lat", None, None), P()),
        check_vma=False,
    )
```

profile of v0, /device:TPU:1, one launch (start us, length us, event | category | flops | bytes accessed | tf_op | source)
XLA Modules:
  0.0 878.4 jit_solution(2196621056070245298)
XLA Ops:
  6.6 6.5 all-to-all-start
  13.1 79.9 %psum.49 = f32[]{:T(128)} all-reduce(f32[]{:T(128)} %multiply_reduce_fusion.8), channel_id=1, replica_groups=mesh['slab'=8,'lat'=32] {'slab','lat'}, use_global_device_ids=true, to_apply=%region_3.4 | all-reduce | flops 1 | bytes 8 | tf_op jit(solution)/shard_map/psum | solution.py:39
  95.5 4.5 fusion.22
  102.8 4.4 all-to-all-start.2
  107.9 11.6 %all-to-all-done.2 = f32[8,32,2,384]{3,2,1,0:T(2,128)S(1)} async-done(((f32[8,32,2,384]{3,2,1,0:T(2,128)}), f32[8,32,2,384]{3,2,1,0:T(2,128)S(1)}, u32[]{:S(2)}, u32[]{:S(2)}) %all-to-all-start.2) | async-done | bytes 786464 | tf_op jit(solution)/shard_map/all_to_all | solution.py:84
  119.5 5.1 all-to-all-start.1
  125.8 7.5 all-to-all-done.1
  138.2 18.7 %all-to-all-done.3 = f32[8,32,2,384]{3,2,0,1:T(2,128)S(1)} async-done(((f32[8,32,2,384]{3,2,0,1:T(2,128)}), f32[8,32,2,384]{3,2,0,1:T(2,128)S(1)}, u32[]{:S(2)}, u32[]{:S(2)}) %all-to-all-start.3) | async-done | bytes 786464 | tf_op jit(solution)/shard_map/all_to_all | solution.py:83
  159.1 77.0 %psum.50 = f32[]{:T(128)} all-reduce(f32[]{:T(128)} %get-tuple-element.34), channel_id=1, replica_groups=mesh['slab'=8,'lat'=32] {'slab','lat'}, use_global_device_ids=true, to_apply=%region_6.7 | all-reduce | flops 1 | bytes 8 | tf_op jit(solution)/shard_map/psum | solution.py:39
  239.6 11.3 %all_to_all.70 = bf16[8,32,2,384]{3,2,1,0:T(2,128)(2,1)S(1)} all-to-all(bf16[8,32,2,384]{3,2,1,0:T(2,128)(2,1)S(1)} %broadcast_select_fusion.2), channel_id=1, replica_groups=mesh['slab'=8,'lat'=32] {'slab'}, dimensions={0} | all-to-all | bytes 786432 | tf_op jit(solution)/shard_map/all_to_all | solution.py:120
  252.0 5.0 all-to-all-start.5
  264.7 4.2 collective-permute-start.3
  272.3 6.1 fusion
  280.4 81.9 %psum.51 = f32[]{:T(128)} all-reduce(f32[]{:T(128)S(6)} %add.322), channel_id=1, replica_groups=mesh['slab'=8,'lat'=32] {'slab','lat'}, use_global_device_ids=true, to_apply=%region_10.11 | all-reduce | flops 1 | bytes 8 | tf_op jit(solution)/shard_map/psum | solution.py:39
  363.0 4.5 fusion.20
  369.5 15.7 %all_to_all.71 = f32[8,32,2,384]{3,2,1,0:T(2,128)S(1)} all-to-all(f32[8,32,2,384]{3,2,1,0:T(2,128)S(1)} %reshape.470), channel_id=1, replica_groups=mesh['slab'=8,'lat'=32] {'slab'}, dimensions={0} | all-to-all | bytes 1572864 | tf_op jit(solution)/shard_map/all_to_all | solution.py:84
  386.4 6.7 all-to-all-start.7
  406.0 8.1 all-to-all-done.7
  416.4 75.8 %psum.52 = f32[]{:T(128)} all-reduce(f32[]{:T(128)} %get-tuple-element.36), channel_id=1, replica_groups=mesh['slab'=8,'lat'=32] {'slab','lat'}, use_global_device_ids=true, to_apply=%region_13.14 | all-reduce | flops 1 | bytes 8 | tf_op jit(solution)/shard_map/psum | solution.py:39
  495.7 11.4 %all_to_all.72 = bf16[8,32,2,384]{3,2,1,0:T(2,128)(2,1)S(1)} all-to-all(bf16[8,32,2,384]{3,2,1,0:T(2,128)(2,1)S(1)} %broadcast_select_fusion.1), channel_id=1, replica_groups=mesh['slab'=8,'lat'=32] {'slab'}, dimensions={0} | all-to-all | bytes 786432 | tf_op jit(solution)/shard_map/all_to_all | solution.py:120
  508.1 5.2 all-to-all-start.9
  528.6 6.1 fusion.1
  536.7 81.9 %psum.53 = f32[]{:T(128)} all-reduce(f32[]{:T(128)S(6)} %add.337), channel_id=1, replica_groups=mesh['slab'=8,'lat'=32] {'slab','lat'}, use_global_device_ids=true, to_apply=%region_17.18 | all-reduce | flops 1 | bytes 8 | tf_op jit(solution)/shard_map/psum | solution.py:39
  619.4 4.5 fusion.18
  625.8 15.7 %all_to_all.73 = f32[8,32,2,384]{3,2,1,0:T(2,128)S(1)} all-to-all(f32[8,32,2,384]{3,2,1,0:T(2,128)S(1)} %reshape.476), channel_id=1, replica_groups=mesh['slab'=8,'lat'=32] {'slab'}, dimensions={0} | all-to-all | bytes 1572864 | tf_op jit(solution)/shard_map/all_to_all | solution.py:84
  642.7 6.7 all-to-all-start.11
  662.4 8.1 all-to-all-done.11
  672.7 75.8 %psum.54 = f32[]{:T(128)} all-reduce(f32[]{:T(128)} %get-tuple-element.38), channel_id=1, replica_groups=mesh['slab'=8,'lat'=32] {'slab','lat'}, use_global_device_ids=true, to_apply=%region_20.21 | all-reduce | flops 1 | bytes 8 | tf_op jit(solution)/shard_map/psum | solution.py:39
  752.0 11.7 %all_to_all.74 = bf16[8,32,2,384]{3,2,1,0:T(2,128)(2,1)S(1)} all-to-all(bf16[8,32,2,384]{3,2,1,0:T(2,128)(2,1)S(1)} %broadcast_select_fusion), channel_id=1, replica_groups=mesh['slab'=8,'lat'=32] {'slab'}, dimensions={0} | all-to-all | bytes 786432 | tf_op jit(solution)/shard_map/all_to_all | solution.py:120
  764.7 5.2 all-to-all-start.13
  785.2 6.1 fusion.2
  793.3 81.9 %psum.55 = f32[]{:T(128)} all-reduce(f32[]{:T(128)S(6)} %add.353), channel_id=1, replica_groups=mesh['slab'=8,'lat'=32] {'slab','lat'}, use_global_device_ids=true, to_apply=%region_24.25 | all-reduce | flops 1 | bytes 8 | tf_op jit(solution)/shard_map/psum | solution.py:39
  (150 shorter events, 110.4 us)
Async XLA Ops:
  6.6 96.2 %all-to-all-start = ((s32[8,32,2]{1,2,0:T(2,128)}), s32[8,32,2]{1,2,0:T(2,128)S(1)}, u32[]{:S(2)}, u32[]{:S(2)}) async-start(s32[8,32,2]{1,2,0:T(2,128)} %copy.100), calls=%async_computation | async-start | bytes 16384 | tf_op jit(solution)/shard_map/all_to_all | solution.py:71
  102.8 16.7 %all-to-all-start.2 = ((f32[8,32,2,384]{3,2,1,0:T(2,128)}), f32[8,32,2,384]{3,2,1,0:T(2,128)S(1)}, u32[]{:S(2)}, u32[]{:S(2)}) async-start(f32[8,32,2,384]{3,2,1,0:T(2,128)} %reshape.464), calls=%async_computation.2 | async-start | bytes 1572864 | tf_op jit(solution)/shard_map/all_to_all | solution.py:84
  119.5 13.8 %all-to-all-start.1 = ((s32[8,32,2]{0,2,1:T(2,128)}), s32[8,32,2]{0,2,1:T(2,128)S(1)}, u32[]{:S(2)}, u32[]{:S(2)}) async-start(s32[8,32,2]{0,2,1:T(2,128)} %copy.101), calls=%async_computation.1 | async-start | bytes 65536 | tf_op jit(solution)/shard_map/all_to_all | solution.py:70
  133.3 23.6 %all-to-all-start.3 = ((f32[8,32,2,384]{3,2,0,1:T(2,128)}), f32[8,32,2,384]{3,2,0,1:T(2,128)S(1)}, u32[]{:S(2)}, u32[]{:S(2)}) async-start(f32[8,32,2,384]{3,2,0,1:T(2,128)} %copy.104), calls=%async_computation.3 | async-start | bytes 1572864 | tf_op jit(solution)/shard_map/all_to_all | solution.py:83
  159.1 113.1 %copy-start = (f32[12,16,3,128]{3,1,2,0:T(8,128)S(1)}, f32[12,16,3,128]{3,1,2,0:T(8,128)}, u32[]{:S(2)}) copy-start(f32[12,16,3,128]{3,1,2,0:T(8,128)} %param.6) | copy-start | bytes 884740
  252.0 26.5 %copy-start.1 = (f32[12,128]{1,0:T(8,128)S(1)}, f32[12,128]{1,0:T(8,128)}, u32[]{:S(2)}) copy-start(f32[12,128]{1,0:T(8,128)} %param.8) | copy-start | bytes 18436
  252.0 18.8 %all-to-all-start.5 = ((bf16[8,32,2,384]{3,2,0,1:T(2,128)(2,1)}), bf16[8,32,2,384]{3,2,0,1:T(2,128)(2,1)S(1)}, u32[]{:S(2)}, u32[]{:S(2)}) async-start(bf16[8,32,2,384]{3,2,0,1:T(2,128)(2,1)} %copy.111), calls=%async_computation.5 | async-start | bytes 786432 | tf_op jit(solution)/shard_map/all_to_all | solution.py:119
  257.0 5.6 collective-permute-start
  260.0 3.3 collective-permute-start.1
  263.4 5.5 collective-permute-start.2
  264.7 4.8 collective-permute-start.3
  386.4 27.8 %all-to-all-start.7 = ((f32[8,32,2,384]{3,2,0,1:T(2,128)}), f32[8,32,2,384]{3,2,0,1:T(2,128)S(1)}, u32[]{:S(2)}, u32[]{:S(2)}) async-start(f32[8,32,2,384]{3,2,0,1:T(2,128)} %copy.115), calls=%async_computation.7 | async-start | bytes 1572864 | tf_op jit(solution)/shard_map/all_to_all | solution.py:83
  393.1 5.6 collective-permute-start.4
  396.4 3.2 collective-permute-start.5
  399.6 5.3 collective-permute-start.6
  400.9 4.9 collective-permute-start.7
  508.1 19.0 %all-to-all-start.9 = ((bf16[8,32,2,384]{3,2,0,1:T(2,128)(2,1)}), bf16[8,32,2,384]{3,2,0,1:T(2,128)(2,1)S(1)}, u32[]{:S(2)}, u32[]{:S(2)}) async-start(bf16[8,32,2,384]{3,2,0,1:T(2,128)(2,1)} %copy.118), calls=%async_computation.9 | async-start | bytes 786432 | tf_op jit(solution)/shard_map/all_to_all | solution.py:119
  513.3 5.6 collective-permute-start.8
  516.4 3.3 collective-permute-start.9
  519.7 5.3 collective-permute-start.10
  521.0 4.8 collective-permute-start.11
  642.7 27.8 %all-to-all-start.11 = ((f32[8,32,2,384]{3,2,0,1:T(2,128)}), f32[8,32,2,384]{3,2,0,1:T(2,128)S(1)}, u32[]{:S(2)}, u32[]{:S(2)}) async-start(f32[8,32,2,384]{3,2,0,1:T(2,128)} %copy.122), calls=%async_computation.11 | async-start | bytes 1572864 | tf_op jit(solution)/shard_map/all_to_all | solution.py:83
  649.5 5.6 collective-permute-start.12
  652.7 3.2 collective-permute-start.13
  655.9 5.3 collective-permute-start.14
  657.2 4.9 collective-permute-start.15
  764.7 19.0 %all-to-all-start.13 = ((bf16[8,32,2,384]{3,2,0,1:T(2,128)(2,1)}), bf16[8,32,2,384]{3,2,0,1:T(2,128)(2,1)S(1)}, u32[]{:S(2)}, u32[]{:S(2)}) async-start(bf16[8,32,2,384]{3,2,0,1:T(2,128)(2,1)} %copy.125), calls=%async_computation.13 | async-start | bytes 786432 | tf_op jit(solution)/shard_map/all_to_all | solution.py:119
  769.9 5.6 collective-permute-start.16
  773.0 3.3 collective-permute-start.17
  776.3 5.7 collective-permute-start.18
  777.6 4.8 collective-permute-start.19
where the time goes:
time: 889 us; the launch traced here: 878 us
  blocking collectives  620 us (70%)
  starting transfers between devices  103 us (12%)
  waiting for transfers between devices  62 us (7%)
  matrix products  35.4 us (4%)
  local copies, waits for them, and re-layouts  32.3 us (4%)
  between operations  13 us (1%)
  other arithmetic  12.5 us (1%)
    psum x7, blocking collectives, total_sum(): return lax.psum(value, ('slab', 'lat'))  554 us
    all_to_all x3, waiting for transfers between devices, deliver(): lax.all_to_all(lax.all_to_all(outgoing, 'slab', split_axis=0, concat_axis...  34.9 us
    all_to_all x3, blocking collectives, shards(): lax.all_to_all(answer, 'slab', split_axis=0, concat_axis=0, tiled=True)  34.4 us
    ppermute x10, starting transfers between devices, extended(): lax.ppermute(lax.slice_in_dim(block, block.shape[dim] - width, None, axis...  32.3 us
    all_to_all x2, blocking collectives, deliver(): lax.all_to_all(outgoing, 'slab', split_axis=0, concat_axis=0, tiled=True)  31.5 us
    ppermute x10, starting transfers between devices, extended(): lax.ppermute(lax.slice_in_dim(block, 0, width, axis=dim), axis, backward)  22.1 us
    dot_general x3, matrix products, shards(): jnp.einsum('tkac,tkpc->tkpa', weights, fetched, preferred_element_type=jn...  18.4 us
  transfers between devices with their start and end apart: 29, of which 18 were waited for; matrix products, arithmetic and copies ran while one was open for 2% of the time, Pallas kernels for 0%

commit v1 on v0

v1 whole, which is shorter than its diff:
```python
import functools

import jax
import jax.numpy as jnp
from jax import lax
from jax.experimental import pallas as pl
from jax.experimental.pallas import tpu as pltpu
from jax.sharding import PartitionSpec as P

MESH = pl.DeviceIdType.MESH
F32 = jnp.float32
BF16 = jnp.bfloat16

TILES = 12
BLOCKS = 16
ENTRIES = TILES * BLOCKS
DEVICES = 256
N_SLAB = 8
N_LAT = 32
SLOTS = 2 * DEVICES
LOCAL = 64
ROW = 384
ITERS = 3
GROUPS = 4
GROUP = DEVICES // GROUPS
EXCHANGES = 2 * ITERS
HALOS = EXCHANGES - 1
SUMS = EXCHANGES + 1
LAM = 0.3
EPS = 1e-6


def dot(a, b):
    return lax.dot_general(a, b, (((1,), (0,)), ((), ())), preferred_element_type=F32)


def iota(shape, dim):
    return lax.broadcasted_iota(jnp.int32, shape, dim).astype(F32)


def one_hot(same):
    return jnp.where(same, 1.0, 0.0).astype(BF16)


def wait_bytes(ref, sem):
    pltpu.make_async_copy(ref, ref, sem).wait()


def block_diagonal(rows):
    place = lax.broadcasted_iota(jnp.int32, rows.shape, 0) % BLOCKS
    empty = jnp.zeros_like(rows)
    return jnp.concatenate([jnp.where(place == k, rows, empty) for k in range(BLOCKS)], axis=1)


def kernel(
    w_hbm, ang_ref, ids_ref, obs_ref, cnt_ref, out_ref, ratio_ref,
    W, WT, S, ST, STL, PICK, PICKT, RAY, TRAV, PART, FETCH, LIVE,
    X0, R0, X, R, V, FACE, HALO, AX, AY, AZ,
    wsem, xsend, xrecv, hsend, hrecv, s1, r1, s2, r2, entered,
):
    s, l = lax.axis_index("slab"), lax.axis_index("lat")
    me = s * N_LAT + l
    y, c, z, x = lax.div(s, 2), lax.rem(s, 2), lax.div(l, 4), lax.rem(l, 4)
    a_me, b_me = z * 2 + c, y * 4 + x

    def a_dev(j):
        return (y * 2 + lax.rem(j, 2), lax.div(j, 2) * 4 + x)

    def b_dev(j):
        return (lax.div(j, 4) * 2 + c, z * 4 + lax.rem(j, 4))

    for t in range(TILES):
        pltpu.make_async_copy(w_hbm.at[t], W.at[t], wsem.at[t]).start()

    barrier = pltpu.get_barrier_semaphore()

    @pl.loop(1, 16)
    def _(j):
        pl.semaphore_signal(barrier, inc=1, device_id=a_dev(lax.rem(a_me + j, 16)), device_id_type=MESH)
        pl.semaphore_signal(barrier, inc=1, device_id=b_dev(lax.rem(b_me + j, 16)), device_id_type=MESH)

    ids = ids_ref[...]
    depth, cross = ids >> 8, ids & 255
    owner = ((depth >> 3) * N_LAT + (cross >> 3) - me) & 255
    inner = (depth & 7) * 8 + (cross & 7)
    owner_r, inner_r = owner.astype(F32), inner.astype(F32)
    square = (ENTRIES, ENTRIES)
    i0, i1 = iota(square, 0), iota(square, 1)

    def column(row):
        return jnp.sum(jnp.where(i0 == i1, row, 0.0), axis=1, keepdims=True)

    owner_c, inner_c = column(owner_r), column(inner_r)
    same = jnp.where(owner_r == owner_c, 1.0, 0.0)
    slot_c = 2.0 * owner_c + jnp.sum(jnp.where(i1 < i0, same, 0.0), axis=1, keepdims=True)
    slot_r = 2.0 * owner_r + jnp.sum(jnp.where(i0 < i1, same, 0.0), axis=0, keepdims=True)
    alone = jnp.sum(same, axis=0, keepdims=True) == 1.0
    spare_r = jnp.where(alone, slot_r + 1.0, -1.0)
    S[...] = one_hot(iota((ENTRIES, SLOTS), 1) == slot_c)
    st = one_hot(iota((SLOTS, ENTRIES), 0) == slot_r)
    stl = one_hot(iota((SLOTS, ENTRIES), 0) == spare_r)
    ST[...] = st
    STL[...] = stl
    wanted = dot(st + stl, one_hot(iota((ENTRIES, 128), 1) == inner_c)).astype(BF16)

    at = iota((TILES, 128), 0) * 128.0 + iota((TILES, 128), 1)
    LIVE[...] = jnp.where(at < cnt_ref[0, 0].astype(F32), 1.0, 0.0)

    def total_row(values):
        return jnp.sum(values, axis=0, keepdims=True)

    def sum_first(n, row):
        AX[n, 0] = row
        AY[n, a_me] = row

        @pl.loop(1, 16)
        def _(j):
            pltpu.make_async_remote_copy(
                AX.at[n, 0], AY.at[n, a_me], s1.at[n], r1.at[n],
                device_id=a_dev(lax.rem(a_me + j, 16)), device_id_type=MESH,
            ).start()

    def sum_second(n):
        wait_bytes(AY.at[n, pl.ds(0, 15)], r1.at[n])
        row = jnp.sum(AY[n], axis=0)
        AX[n, 1] = row
        AZ[n, b_me] = row

        @pl.loop(1, 16)
        def _(j):
            pltpu.make_async_remote_copy(
                AX.at[n, 1], AZ.at[n, b_me], s2.at[n], r2.at[n],
                device_id=b_dev(lax.rem(b_me + j, 16)), device_id_type=MESH,
            ).start()

    def sum_third(n):
        wait_bytes(AZ.at[n, pl.ds(0, 15)], r2.at[n])
        total = jnp.sum(jnp.sum(AZ[n], axis=0), axis=1, keepdims=True)
        return jnp.sqrt(jnp.broadcast_to(total, (1, 128)) + EPS)

    def buffers(e):
        return (X0, R0) if e == 0 else (X.at[e - 1], R.at[e - 1])

    def send_group(e, g, forward):
        src, dst = buffers(e)

        def send(j):
            d = lax.rem(me + j if forward else me + DEVICES - j, DEVICES)
            pltpu.make_async_remote_copy(
                src.at[j], dst.at[j], xsend.at[e], xrecv.at[e, g],
                device_id=(lax.div(d, N_LAT), lax.rem(d, N_LAT)), device_id_type=MESH,
            ).start()

        if g == 0:
            pltpu.make_async_copy(src.at[0], dst.at[0], xrecv.at[e, 0]).start()

        @pl.loop(max(g * GROUP, 1), (g + 1) * GROUP)
        def _(j):
            send(j)

    def receive_group(e, g):
        dst = buffers(e)[1].at[pl.ds(g * GROUP, GROUP)]
        wait_bytes(dst, xrecv.at[e, g])
        return dst[...].reshape(2 * GROUP, dst.shape[-1])

    def send_halo(h):
        for p in range(3):
            v = V[h, p]
            FACE[h, 0, p] = jnp.concatenate([v[8 * i:8 * i + 1] for i in range(8)], axis=0)
            FACE[h, 1, p] = jnp.concatenate([v[8 * i + 7:8 * i + 8] for i in range(8)], axis=0)
        before, after = lax.rem(s + N_SLAB - 1, N_SLAB), lax.rem(s + 1, N_SLAB)
        left, right = lax.rem(l + N_LAT - 1, N_LAT), lax.rem(l + 1, N_LAT)
        moves = (
            (V.at[h, :, pl.ds(56, 8)], 0, (after, l)),
            (V.at[h, :, pl.ds(0, 8)], 1, (before, l)),
            (FACE.at[h, 1], 2, (s, right)),
            (FACE.at[h, 0], 3, (s, left)),
        )
        for src, side, device in moves:
            pltpu.make_async_remote_copy(
                src, HALO.at[h, side], hsend.at[h, side], hrecv.at[h, side],
                device_id=device, device_id_type=MESH,
            ).start()

    def laplace(h):
        for side in range(4):
            wait_bytes(HALO.at[h, side], hrecv.at[h, side])
        row = lax.broadcasted_iota(jnp.int32, (LOCAL, 128), 0) % 8
        lane = lax.broadcasted_iota(jnp.int32, (LOCAL, 128), 1)

        def spread(face):
            return jnp.concatenate([jnp.broadcast_to(face[i:i + 1], (8, 128)) for i in range(8)], axis=0)

        result = []
        for p in range(3):
            v = V[h, p]
            low = jnp.where(s > 0, HALO[h, 0, p], 0.0)
            high = jnp.where(s < N_SLAB - 1, HALO[h, 1, p], 0.0)
            left = jnp.where(l > 0, HALO[h, 2, p], 0.0)
            right = jnp.where(l < N_LAT - 1, HALO[h, 3, p], 0.0)
            beside = jnp.concatenate([low, v[:56]], axis=0) + jnp.concatenate([v[8:], high], axis=0)
            beside = beside + jnp.where(row == 0, spread(left), pltpu.roll(v, 1, 0))
            beside = beside + jnp.where(row == 7, spread(right), pltpu.roll(v, LOCAL - 1, 0))
            beside = beside + jnp.where(lane == 0, 0.0, pltpu.roll(v, 1, 1))
            beside = beside + jnp.where(lane == 127, 0.0, pltpu.roll(v, 127, 1))
            result.append(6.0 * v - beside)
        return result

    def adjoint(first):
        def tile(t, carry):
            if first:
                wait_bytes(W.at[t], wsem.at[t])
            weighted = ang_ref[t] * RAY[pl.ds(t, 1), :]
            high = weighted.astype(BF16)
            low = (weighted - high.astype(F32)).astype(BF16)
            rows = block_diagonal(jnp.concatenate([high, low], axis=0))
            out = dot(rows, W[t].reshape(BLOCKS * 128, 128))
            out = out[:48] + out[48:]
            for p in range(3):
                PART[p, pl.ds(pl.multiple_of(t * BLOCKS, BLOCKS), BLOCKS), :] = out[p * BLOCKS:(p + 1) * BLOCKS]
            return carry

        lax.fori_loop(0, TILES, tile, 0, unroll=2)

    def send_adjoint(e):
        high = [PART[p].astype(BF16) for p in range(3)]
        low = [(PART[p] - high[p].astype(F32)).astype(BF16) for p in range(3)]
        high, low = jnp.concatenate(high, axis=1), jnp.concatenate(low, axis=1)
        for g in range(GROUPS):
            at = pl.ds(g * 2 * GROUP, 2 * GROUP)
            rows = (dot(ST[at, :], high) + dot(STL[at, :], low)).astype(BF16)
            if e == 0:
                rows = jnp.concatenate([rows, wanted[g * 2 * GROUP:(g + 1) * 2 * GROUP]], axis=1)
            src = buffers(e)[0]
            src[pl.ds(g * GROUP, GROUP)] = rows.reshape(GROUP, 2, rows.shape[-1])
            if g == GROUPS - 1:
                sum_second(e)
            send_group(e, g, True)

    def send_forward(e, model):
        model = jnp.concatenate(model, axis=1).astype(BF16)
        for g in range(GROUPS):
            rows = dot(PICK[pl.ds(g * 2 * GROUP, 2 * GROUP), :], model).astype(BF16)
            buffers(e)[0][pl.ds(g * GROUP, GROUP)] = rows.reshape(GROUP, 2, ROW)
            if g == GROUPS - 1:
                sum_second(e)
            send_group(e, g, False)

    def collect(e):
        total = None
        for g in range(GROUPS):
            rows = receive_group(e, g)
            part = dot(PICKT[g], rows)
            total = part if total is None else total + part
        return [total[:, p * 128:(p + 1) * 128] for p in range(3)]

    def travel(e):
        total = None
        for g in range(GROUPS):
            rows = receive_group(e, g)
            part = dot(S[:, pl.ds(g * 2 * GROUP, 2 * GROUP)], rows)
            total = part if total is None else total + part
        FETCH[...] = total.astype(BF16)

        def tile(t, carry):
            at = pl.ds(pl.multiple_of(t * BLOCKS, BLOCKS), BLOCKS)
            rows = jnp.concatenate([FETCH[at, p * 128:(p + 1) * 128] for p in range(3)], axis=0)
            out = dot(block_diagonal(rows), WT[t]) * ang_ref[t]
            TRAV[pl.ds(t, 1), :] = jnp.sum(out, axis=0, keepdims=True)
            return carry

        lax.fori_loop(0, TILES, tile, 0, unroll=2)
        return TRAV[...]

    ray = obs_ref[...] * LIVE[...]
    RAY[...] = ray
    adjoint(True)
    pl.semaphore_wait(barrier, 30)

    @pl.loop(1, 16)
    def _(j):
        pl.semaphore_signal(entered, inc=1, device_id=b_dev(lax.rem(b_me + j, 16)), device_id_type=MESH)

    pl.semaphore_wait(entered, 15)
    sum_first(0, total_row(ray * ray))
    send_adjoint(0)

    def turn(t, carry):
        for k in range(BLOCKS):
            WT[t, k * 128:(k + 1) * 128, :] = W[t, k].T
        return carry

    lax.fori_loop(0, TILES, turn, 0)
    norm = sum_third(0)
    first_norm = norm
    ray = ray / norm
    total = None
    for g in range(GROUPS):
        rows = receive_group(0, g)
        pick = rows[:, ROW:ROW + LOCAL]
        PICK[pl.ds(g * 2 * GROUP, 2 * GROUP), :] = pick
        PICKT[g] = pick.T
        part = dot(PICKT[g], rows[:, :ROW])
        total = part if total is None else total + part
    model_raw = [total[:, p * 128:(p + 1) * 128] / norm for p in range(3)]

    cell = [jnp.zeros((LOCAL, 128), F32) for _ in range(3)]
    direction = None
    phi_bar = first_norm
    rho_bar = u_norm = rho_now = sin_term = cos_term = None
    result = [jnp.zeros((LOCAL, 128), F32) for _ in range(3)]
    for i in range(ITERS):
        e = 2 * i + 1
        for p in range(3):
            V[e - 1, p] = model_raw[p]
        sum_first(e, total_row(sum(v * v for v in model_raw)))
        send_halo(e - 1)
        send_forward(e, model_raw)
        smooth = laplace(e - 1)
        v_norm = sum_third(e)
        model = [v / v_norm for v in model_raw]
        if i == 0:
            rho_bar = v_norm
            direction = model
        else:
            theta = sin_term * v_norm
            rho_bar = -cos_term * v_norm
            direction = [m - theta / rho_now * d for m, d in zip(model, direction)]
        cell_raw = [LAM * sm / v_norm - v_norm * q for sm, q in zip(smooth, cell)]
        cell_sum = total_row(sum(q * q for q in cell_raw))
        if i < ITERS - 1:
            for p in range(3):
                V[e, p] = cell_raw[p]
        ray_raw = travel(e) * LIVE[...] / v_norm - v_norm * ray
        sum_first(e + 1, cell_sum + total_row(ray_raw * ray_raw))
        if i < ITERS - 1:
            send_halo(e)
            RAY[...] = ray_raw
            adjoint(False)
            send_adjoint(e + 1)
            smooth = laplace(e)
        else:
            sum_second(e + 1)
        u_norm = sum_third(e + 1)
        rho_now = jnp.sqrt(rho_bar * rho_bar + u_norm * u_norm)
        cos_term = rho_bar / rho_now
        sin_term = u_norm / rho_now
        phi_now = cos_term * phi_bar
        phi_bar = sin_term * phi_bar
        result = [r + phi_now / rho_now * d for r, d in zip(result, direction)]
        if i < ITERS - 1:
            ray = ray_raw / u_norm
            cell = [q / u_norm for q in cell_raw]
            back = collect(e + 1)
            model_raw = [
                b / u_norm + LAM * sm / u_norm - u_norm * m for b, sm, m in zip(back, smooth, model)
            ]

    for p in range(3):
        out_ref[p] = result[p]
    ratio_ref[...] = phi_bar / first_norm

    for e in range(EXCHANGES):
        wait_bytes(buffers(e)[0].at[pl.ds(0, DEVICES - 1)], xsend.at[e])
    for h in range(HALOS):
        for side in range(4):
            wait_bytes(HALO.at[h, side], hsend.at[h, side])
    for n in range(SUMS):
        wait_bytes(AY.at[n, pl.ds(0, 15)], s1.at[n])
        wait_bytes(AZ.at[n, pl.ds(0, 15)], s2.at[n])


def shards(weights, angles, block_list, observed, ray_count):
    ids = block_list.reshape(1, ENTRIES)
    ang = angles.transpose(0, 2, 1, 3).reshape(TILES, 3 * BLOCKS, 128)
    vmem = pl.BlockSpec(memory_space=pltpu.VMEM)
    dma = pltpu.SemaphoreType.DMA
    out, ratio = pl.pallas_call(
        kernel,
        out_shape=(
            jax.ShapeDtypeStruct((3, LOCAL, 128), F32),
            jax.ShapeDtypeStruct((1, 128), F32),
        ),
        in_specs=[pl.BlockSpec(memory_space=pl.ANY), vmem, vmem, vmem, pl.BlockSpec(memory_space=pltpu.SMEM)],
        out_specs=(vmem, vmem),
        scratch_shapes=[
            pltpu.VMEM((TILES, BLOCKS, 128, 128), BF16),
            pltpu.VMEM((TILES, BLOCKS * 128, 128), BF16),
            pltpu.VMEM((ENTRIES, SLOTS), BF16),
            pltpu.VMEM((SLOTS, ENTRIES), BF16),
            pltpu.VMEM((SLOTS, ENTRIES), BF16),
            pltpu.VMEM((SLOTS, LOCAL), BF16),
            pltpu.VMEM((GROUPS, LOCAL, 2 * GROUP), BF16),
            pltpu.VMEM((TILES, 128), F32),
            pltpu.VMEM((TILES, 128), F32),
            pltpu.VMEM((3, ENTRIES, 128), F32),
            pltpu.VMEM((ENTRIES, ROW), BF16),
            pltpu.VMEM((TILES, 128), F32),
            pltpu.VMEM((DEVICES, 2, ROW + 128), BF16),
            pltpu.VMEM((DEVICES, 2, ROW + 128), BF16),
            pltpu.VMEM((EXCHANGES - 1, DEVICES, 2, ROW), BF16),
            pltpu.VMEM((EXCHANGES - 1, DEVICES, 2, ROW), BF16),
            pltpu.VMEM((HALOS, 3, LOCAL, 128), F32),
            pltpu.VMEM((HALOS, 2, 3, 8, 128), F32),
            pltpu.VMEM((HALOS, 4, 3, 8, 128), F32),
            pltpu.VMEM((SUMS, 2, 1, 128), F32),
            pltpu.VMEM((SUMS, 16, 1, 128), F32),
            pltpu.VMEM((SUMS, 16, 1, 128), F32),
            dma((TILES,)),
            dma((EXCHANGES,)),
            dma((EXCHANGES, GROUPS)),
            dma((HALOS, 4)),
            dma((HALOS, 4)),
            dma((SUMS,)),
            dma((SUMS,)),
            dma((SUMS,)),
            dma((SUMS,)),
            pltpu.SemaphoreType.REGULAR,
        ],
        compiler_params=pltpu.CompilerParams(
            collective_id=0, has_side_effects=True, vmem_limit_bytes=56 * 1024 * 1024
        ),
    )(weights, ang, ids, observed, ray_count)
    out = out.reshape(3, 8, 8, 128).transpose(1, 2, 0, 3)
    return out, ratio[0, 0]


def solution(mesh):
    placed = (
        P(("slab", "lat"), None, None, None),
        P(("slab", "lat"), None, None, None),
        P(("slab", "lat"), None),
        P(("slab", "lat"), None),
        P("slab", "lat"),
    )
    return jax.shard_map(
        shards,
        mesh=mesh,
        in_specs=placed,
        out_specs=(P("slab", "lat", None, None), P()),
        check_vma=False,
    )
```

time: 889 us -> 128 us (0.14); the launches traced: 878 us -> 128 us
  blocking collectives: 620 us -> 0 us
  Pallas kernels: 0 us -> 122 us
  starting transfers between devices: 103 us -> 0 us
  waiting for transfers between devices: 62 us -> 0 us
  matrix products: 35.4 us -> 0 us
  local copies, waits for them, and re-layouts: 32.3 us -> 2.88 us
  other arithmetic: 12.5 us -> 0 us
  between operations: 13 us -> 3.1 us
    psum x7 -> x0, blocking collectives: 554 us -> none  [total_sum(): return lax.psum(value, ('slab', 'lat'))]
    pallas_call x0 -> x1, Pallas kernels: none -> 122 us  [shards(): pl.pallas_call(kernel, out_shape=(jax.ShapeDtypeStruct((3, LOCAL, 128), F...]
    all_to_all x5 -> x0, blocking collectives: 65.9 us -> none  [the longest x3 34.4 us: shards(): lax.all_to_all(answer, 'slab', split_axis=0, concat_axis=0, tiled=True)]
    all_to_all x9 -> x0, waiting for transfers between devices: 54.4 us -> none  [the longest x3 34.9 us: deliver(): lax.all_to_all(lax.all_to_all(outgoing, 'slab', split_axis=0, concat_axis...]
    ppermute x20 -> x0, starting transfers between devices: 54.4 us -> none  [the longest x10 32.3 us: extended(): lax.ppermute(lax.slice_in_dim(block, block.shape[dim] - width, None, axis...]
    all_to_all x9 -> x0, starting transfers between devices: 48.6 us -> none  [the longest x3 17.4 us: deliver(): lax.all_to_all(lax.all_to_all(outgoing, 'slab', split_axis=0, concat_axis...]
    dot_general x9 -> x0, matrix products: 35.4 us -> none  [the longest x3 18.4 us: shards(): jnp.einsum('tkac,tkpc->tkpa', weights, fetched, preferred_element_type=jn...]
    gather x9 -> x0, local copies, waits for them, and re-layouts: 9.3 us -> none  [the longest x6 6.26 us: shards(): rows_local[jnp.clip(requested, 0, local_blocks - 1)]]
  transfers between devices with their start and end apart: 29 -> 0, of which waited for: 18 -> 0; matrix products, arithmetic and copies ran while one was open for 2% -> 0% of each run, Pallas kernels for 0% -> 0%
where the time goes in v1:
time: 128 us
  Pallas kernels  122 us (95%)
  between operations  3.1 us (2%)
  local copies, waits for them, and re-layouts  2.88 us (2%)
    pallas_call x1, Pallas kernels, shards(): pl.pallas_call(kernel, out_shape=(jax.ShapeDtypeStruct((3, LOCAL, 128), F...  122 us

profile of v1, /device:TPU:1, one launch (start us, length us, event | category | flops | bytes accessed | tf_op | source)
XLA Modules:
  0.0 127.8 jit_solution(15720982482285070839)
XLA Ops:
  1.3 1.3 %reshape.14.ids_ref = s32[1,192]{1,0:T(1,128)} reshape(s32[12,16]{1,0:T(8,128)} %param.7) | data formatting | bytes 1536 | tf_op jit(solution)/shard_map/reshape | solution.py:374
  2.6 121.8 %shard_map.68 = (f32[3,64,128]{2,1,0:T(8,128)}, f32[1,128]{1,0:T(1,128)}) custom-call(bf16[12,16,128,128]{3,2,1,0:T(8,128)(2,1)} %w_hbm.1, f32[12,48,128]{2,1,0:T(8,128)} %bitcast.10, s32[1,192]{1,0:T(1,128)} %reshape.14.ids_ref, f32[12,128]{1,0:T(8,128)} %obs_ref.1, s32[1,1]{1,0:T(1,128)S(6)} %copy.10.cnt_ref), custom_call_target="tpu_custom_call" | custom-call | tf_op jit(solution)/shard_map/pallas_call | solution.py:378
  124.4 1.5 %copy_bitcast_fusion = f32[8,8,3,128]{3,1,2,0:T(8,128)} fusion(f32[3,64,128]{2,1,0:T(8,128)} %get-tuple-element.4), kind=kLoop, calls=%fused_computation | loop fusion | bytes 196608 | tf_op jit(solution)/shard_map/transpose | solution.py:424

commit v2 on v1

--- a/solution.py
+++ b/solution.py
@@ -21,7 +21,9 @@
 LOCAL = 64
 ROW = 384
 ITERS = 3
-GROUPS = 4
+GROUPS = 8
+FAR = (4, 5, 3, 6)
+NEAR = (2, 7, 1, 0)
 GROUP = DEVICES // GROUPS
 EXCHANGES = 2 * ITERS
 HALOS = EXCHANGES - 1
@@ -54,7 +56,7 @@
 
 def kernel(
     w_hbm, ang_ref, ids_ref, obs_ref, cnt_ref, out_ref, ratio_ref,
-    W, WT, S, ST, STL, PICK, PICKT, RAY, TRAV, PART, FETCH, LIVE,
+    W, WT, S, ST, STL, PICK, PICKT, RAY, PART, FETCH, LIVE,
     X0, R0, X, R, V, FACE, HALO, AX, AY, AZ,
     wsem, xsend, xrecv, hsend, hrecv, s1, r1, s2, r2, entered,
 ):
@@ -79,10 +81,34 @@
         pl.semaphore_signal(barrier, inc=1, device_id=a_dev(lax.rem(a_me + j, 16)), device_id_type=MESH)
         pl.semaphore_signal(barrier, inc=1, device_id=b_dev(lax.rem(b_me + j, 16)), device_id_type=MESH)
 
+    spread_k = jnp.where(
+        (lax.broadcasted_iota(jnp.int32, (BLOCKS, ENTRIES), 1) & (BLOCKS - 1))
+        == lax.broadcasted_iota(jnp.int32, (BLOCKS, ENTRIES), 0),
+        1.0, 0.0,
+    ).astype(BF16)
+    own_tile = (lax.broadcasted_iota(jnp.int32, (TILES, ENTRIES), 1) >> 4) == lax.broadcasted_iota(
+        jnp.int32, (TILES, ENTRIES), 0
+    )
+
+    def in_a_row(values):
+        spread = dot(values.astype(F32).astype(BF16), spread_k)
+        return jnp.sum(jnp.where(own_tile, spread, 0.0), axis=0, keepdims=True).astype(jnp.int32)
+
     ids = ids_ref[...]
-    depth, cross = ids >> 8, ids & 255
-    owner = ((depth >> 3) * N_LAT + (cross >> 3) - me) & 255
+    depth, cross = in_a_row(ids >> 8), in_a_row(ids & 255)
     inner = (depth & 7) * 8 + (cross & 7)
+    slab_o, lat_o = depth >> 3, cross >> 3
+    dx, dz = ((lat_o & 3) - x) & 3, ((lat_o >> 2) - z) & 7
+    dy, dc = ((slab_o >> 1) - y) & 3, ((slab_o & 1) - c) & 1
+
+    def far_first(d):
+        return jnp.where(d == 0, 3, jnp.where(d == 1, 2, jnp.where(d == 2, 0, 1)))
+
+    place_z = jnp.zeros_like(dz)
+    for k in range(4):
+        place_z = jnp.where(dz == FAR[k], k, place_z)
+        place_z = jnp.where(dz == NEAR[k], 128 + k, place_z)
+    owner = place_z + 4 * ((far_first(dx) * 4 + far_first(dy)) * 2 + 1 - dc)
     owner_r, inner_r = owner.astype(F32), inner.astype(F32)
     square = (ENTRIES, ENTRIES)
     i0, i1 = iota(square, 0), iota(square, 1)
@@ -96,7 +122,8 @@
     slot_r = 2.0 * owner_r + jnp.sum(jnp.where(i0 < i1, same, 0.0), axis=0, keepdims=True)
     alone = jnp.sum(same, axis=0, keepdims=True) == 1.0
     spare_r = jnp.where(alone, slot_r + 1.0, -1.0)
-    S[...] = one_hot(iota((ENTRIES, SLOTS), 1) == slot_c)
+    for g in range(GROUPS):
+        S[g] = one_hot(iota((ENTRIES, 2 * GROUP), 1) + float(2 * GROUP * g) == slot_c)
     st = one_hot(iota((SLOTS, ENTRIES), 0) == slot_r)
     stl = one_hot(iota((SLOTS, ENTRIES), 0) == spare_r)
     ST[...] = st
@@ -143,20 +170,38 @@
 
     def send_group(e, g, forward):
         src, dst = buffers(e)
-
-        def send(j):
-            d = lax.rem(me + j if forward else me + DEVICES - j, DEVICES)
+        steps = FAR if g < GROUPS // 2 else NEAR
+
+        def offset(i):
+            far = 3 - i
+            return lax.rem(lax.div(far * (far + 1), 2), 4)
+
+        def place(at, d, n):
+            return lax.rem(at + n - d, n) if forward else lax.rem(at + d, n)
+
+        def one(q, k, to_x, to_slab):
+            j = (g // (GROUPS // 2)) * 128 + q * 4 + k
+            to_z = lax.rem(z + (8 - steps[k] if forward else steps[k]), 8)
             pltpu.make_async_remote_copy(
                 src.at[j], dst.at[j], xsend.at[e], xrecv.at[e, g],
-                device_id=(lax.div(d, N_LAT), lax.rem(d, N_LAT)), device_id_type=MESH,
+                device_id=(to_slab, to_z * 4 + to_x), device_id_type=MESH,
             ).start()
 
-        if g == 0:
-            pltpu.make_async_copy(src.at[0], dst.at[0], xrecv.at[e, 0]).start()
-
-        @pl.loop(max(g * GROUP, 1), (g + 1) * GROUP)
-        def _(j):
-            send(j)
+        first = (g % (GROUPS // 2)) * (GROUP // 4)
+        last = first + GROUP // 4
+
+        @pl.loop(first, last - 1 if g == GROUPS - 1 else last)
+        def _(q):
+            to_x = place(x, offset(lax.div(q, 8)), 4)
+            to_y = place(y, offset(lax.rem(lax.div(q, 2), 4)), 4)
+            to_c = lax.rem(c + 1 - lax.rem(q, 2), 2)
+            for k in range(4):
+                one(q, k, to_x, to_y * 2 + to_c)
+
+        if g == GROUPS - 1:
+            for k in range(3):
+                one(31, k, x, s)
+            pltpu.make_async_copy(src.at[DEVICES - 1], dst.at[DEVICES - 1], xrecv.at[e, g]).start()
 
     def receive_group(e, g):
         dst = buffers(e)[1].at[pl.ds(g * GROUP, GROUP)]
@@ -206,23 +251,23 @@
             result.append(6.0 * v - beside)
         return result
 
-    def adjoint(first):
-        def tile(t, carry):
-            if first:
-                wait_bytes(W.at[t], wsem.at[t])
-            weighted = ang_ref[t] * RAY[pl.ds(t, 1), :]
-            high = weighted.astype(BF16)
-            low = (weighted - high.astype(F32)).astype(BF16)
-            rows = block_diagonal(jnp.concatenate([high, low], axis=0))
-            out = dot(rows, W[t].reshape(BLOCKS * 128, 128))
-            out = out[:48] + out[48:]
-            for p in range(3):
-                PART[p, pl.ds(pl.multiple_of(t * BLOCKS, BLOCKS), BLOCKS), :] = out[p * BLOCKS:(p + 1) * BLOCKS]
-            return carry
-
-        lax.fori_loop(0, TILES, tile, 0, unroll=2)
-
-    def send_adjoint(e):
+    def forward_tile(t):
+        rows = jnp.concatenate(
+            [FETCH[t * BLOCKS:(t + 1) * BLOCKS, p * 128:(p + 1) * 128] for p in range(3)], axis=0
+        )
+        return total_row(dot(block_diagonal(rows), WT[t]) * ang_ref[t])
+
+    def adjoint_tile(t, ray_row):
+        weighted = ang_ref[t] * ray_row
+        high = weighted.astype(BF16)
+        low = (weighted - high.astype(F32)).astype(BF16)
+        rows = block_diagonal(jnp.concatenate([high, low], axis=0))
+        out = dot(rows, W[t].reshape(BLOCKS * 128, 128))
+        out = out[:48] + out[48:]
+        for p in range(3):
+            PART[p, t * BLOCKS:(t + 1) * BLOCKS, :] = out[p * BLOCKS:(p + 1) * BLOCKS]
+
+    def send_adjoint(e, after_first):
         high = [PART[p].astype(BF16) for p in range(3)]
         low = [(PART[p] - high[p].astype(F32)).astype(BF16) for p in range(3)]
         high, low = jnp.concatenate(high, axis=1), jnp.concatenate(low, axis=1)
@@ -233,57 +278,43 @@
                 rows = jnp.concatenate([rows, wanted[g * 2 * GROUP:(g + 1) * 2 * GROUP]], axis=1)
             src = buffers(e)[0]
             src[pl.ds(g * GROUP, GROUP)] = rows.reshape(GROUP, 2, rows.shape[-1])
-            if g == GROUPS - 1:
-                sum_second(e)
-            send_group(e, g, True)
-
-    def send_forward(e, model):
+            send_group(e, g, False)
+            if g == 0:
+                after_first()
+        sum_second(e)
+
+    def send_forward(e, model, after_first):
         model = jnp.concatenate(model, axis=1).astype(BF16)
         for g in range(GROUPS):
             rows = dot(PICK[pl.ds(g * 2 * GROUP, 2 * GROUP), :], model).astype(BF16)
             buffers(e)[0][pl.ds(g * GROUP, GROUP)] = rows.reshape(GROUP, 2, ROW)
-            if g == GROUPS - 1:
-                sum_second(e)
-            send_group(e, g, False)
-
-    def collect(e):
-        total = None
-        for g in range(GROUPS):
-            rows = receive_group(e, g)
-            part = dot(PICKT[g], rows)
+            send_group(e, g, True)
+            if g == 0:
+                after_first()
+        sum_second(e)
+
+    def gather(e, table, groups, total=None):
+        for g in groups:
+            part = dot(table[g], receive_group(e, g))
             total = part if total is None else total + part
+        return total
+
+    def by_parameter(total):
         return [total[:, p * 128:(p + 1) * 128] for p in range(3)]
-
-    def travel(e):
-        total = None
-        for g in range(GROUPS):
-            rows = receive_group(e, g)
-            part = dot(S[:, pl.ds(g * 2 * GROUP, 2 * GROUP)], rows)
-            total = part if total is None else total + part
-        FETCH[...] = total.astype(BF16)
-
-        def tile(t, carry):
-            at = pl.ds(pl.multiple_of(t * BLOCKS, BLOCKS), BLOCKS)
-            rows = jnp.concatenate([FETCH[at, p * 128:(p + 1) * 128] for p in range(3)], axis=0)
-            out = dot(block_diagonal(rows), WT[t]) * ang_ref[t]
-            TRAV[pl.ds(t, 1), :] = jnp.sum(out, axis=0, keepdims=True)
-            return carry
-
-        lax.fori_loop(0, TILES, tile, 0, unroll=2)
-        return TRAV[...]
 
     ray = obs_ref[...] * LIVE[...]
     RAY[...] = ray
-    adjoint(True)
     pl.semaphore_wait(barrier, 30)
 
     @pl.loop(1, 16)
     def _(j):
         pl.semaphore_signal(entered, inc=1, device_id=b_dev(lax.rem(b_me + j, 16)), device_id_type=MESH)
 
+    for t in range(TILES):
+        wait_bytes(W.at[t], wsem.at[t])
+        adjoint_tile(t, RAY[t:t + 1, :])
     pl.semaphore_wait(entered, 15)
-    sum_first(0, total_row(ray * ray))
-    send_adjoint(0)
+    send_adjoint(0, lambda: sum_first(0, total_row(ray * ray)))
 
     def turn(t, carry):
         for k in range(BLOCKS):
@@ -291,9 +322,6 @@
         return carry
 
     lax.fori_loop(0, TILES, turn, 0)
-    norm = sum_third(0)
-    first_norm = norm
-    ray = ray / norm
     total = None
     for g in range(GROUPS):
         rows = receive_group(0, g)
@@ -302,21 +330,29 @@
         PICKT[g] = pick.T
         part = dot(PICKT[g], rows[:, :ROW])
         total = part if total is None else total + part
-    model_raw = [total[:, p * 128:(p + 1) * 128] / norm for p in range(3)]
+    first_norm = sum_third(0)
+    ray = ray / first_norm
+    model_raw = [part / first_norm for part in by_parameter(total)]
 
     cell = [jnp.zeros((LOCAL, 128), F32) for _ in range(3)]
-    direction = None
+    direction = model = smooth = None
     phi_bar = first_norm
     rho_bar = u_norm = rho_now = sin_term = cos_term = None
     result = [jnp.zeros((LOCAL, 128), F32) for _ in range(3)]
+    most, rest = range(GROUPS - 1), range(GROUPS - 1, GROUPS)
     for i in range(ITERS):
         e = 2 * i + 1
-        for p in range(3):
-            V[e - 1, p] = model_raw[p]
-        sum_first(e, total_row(sum(v * v for v in model_raw)))
-        send_halo(e - 1)
-        send_forward(e, model_raw)
+        final = i == ITERS - 1
+
+        def beside_forward():
+            for p in range(3):
+                V[e - 1, p] = model_raw[p]
+            sum_first(e, total_row(sum(v * v for v in model_raw)))
+            send_halo(e - 1)
+
+        send_forward(e, model_raw, beside_forward)
         smooth = laplace(e - 1)
+        fetched = gather(e, S, most)
         v_norm = sum_third(e)
         model = [v / v_norm for v in model_raw]
         if i == 0:
@@ -328,18 +364,29 @@
             direction = [m - theta / rho_now * d for m, d in zip(model, direction)]
         cell_raw = [LAM * sm / v_norm - v_norm * q for sm, q in zip(smooth, cell)]
         cell_sum = total_row(sum(q * q for q in cell_raw))
-        if i < ITERS - 1:
+        if not final:
             for p in range(3):
                 V[e, p] = cell_raw[p]
-        ray_raw = travel(e) * LIVE[...] / v_norm - v_norm * ray
-        sum_first(e + 1, cell_sum + total_row(ray_raw * ray_raw))
-        if i < ITERS - 1:
             send_halo(e)
-            RAY[...] = ray_raw
-            adjoint(False)
-            send_adjoint(e + 1)
+        scale = LIVE[...] / v_norm
+        known = v_norm * ray
+        FETCH[...] = gather(e, S, rest, fetched).astype(BF16)
+        for t in range(TILES):
+            row = forward_tile(t) * scale[t:t + 1] - known[t:t + 1]
+            RAY[t:t + 1, :] = row
+            if not final:
+                adjoint_tile(t, row)
+
+        def beside_adjoint():
+            ray_raw = RAY[...]
+            sum_first(e + 1, cell_sum + total_row(ray_raw * ray_raw))
+
+        if not final:
+            send_adjoint(e + 1, beside_adjoint)
             smooth = laplace(e)
+            back = gather(e + 1, PICKT, most)
         else:
+            beside_adjoint()
             sum_second(e + 1)
         u_norm = sum_third(e + 1)
         rho_now = jnp.sqrt(rho_bar * rho_bar + u_norm * u_norm)
@@ -348,13 +395,12 @@
         phi_now = cos_term * phi_bar
         phi_bar = sin_term * phi_bar
         result = [r + phi_now / rho_now * d for r, d in zip(result, direction)]
-        if i < ITERS - 1:
-            ray = ray_raw / u_norm
+        if not final:
+            ray = RAY[...] / u_norm
             cell = [q / u_norm for q in cell_raw]
-            back = collect(e + 1)
-            model_raw = [
-                b / u_norm + LAM * sm / u_norm - u_norm * m for b, sm, m in zip(back, smooth, model)
-            ]
+            known = [LAM * sm / u_norm - u_norm * m for sm, m in zip(smooth, model)]
+            back = gather(e + 1, PICKT, rest, back)
+            model_raw = [b / u_norm + k for b, k in zip(by_parameter(back), known)]
 
     for p in range(3):
         out_ref[p] = result[p]
@@ -371,7 +417,6 @@
 
 
 def shards(weights, angles, block_list, observed, ray_count):
-    ids = block_list.reshape(1, ENTRIES)
     ang = angles.transpose(0, 2, 1, 3).reshape(TILES, 3 * BLOCKS, 128)
     vmem = pl.BlockSpec(memory_space=pltpu.VMEM)
     dma = pltpu.SemaphoreType.DMA
@@ -386,12 +431,11 @@
         scratch_shapes=[
             pltpu.VMEM((TILES, BLOCKS, 128, 128), BF16),
             pltpu.VMEM((TILES, BLOCKS * 128, 128), BF16),
-            pltpu.VMEM((ENTRIES, SLOTS), BF16),
+            pltpu.VMEM((GROUPS, ENTRIES, 2 * GROUP), BF16),
             pltpu.VMEM((SLOTS, ENTRIES), BF16),
             pltpu.VMEM((SLOTS, ENTRIES), BF16),
             pltpu.VMEM((SLOTS, LOCAL), BF16),
             pltpu.VMEM((GROUPS, LOCAL, 2 * GROUP), BF16),
-            pltpu.VMEM((TILES, 128), F32),
             pltpu.VMEM((TILES, 128), F32),
             pltpu.VMEM((3, ENTRIES, 128), F32),
             pltpu.VMEM((ENTRIES, ROW), BF16),
@@ -420,7 +464,7 @@
         compiler_params=pltpu.CompilerParams(
             collective_id=0, has_side_effects=True, vmem_limit_bytes=56 * 1024 * 1024
         ),
-    )(weights, ang, ids, observed, ray_count)
+    )(weights, ang, block_list, observed, ray_count)
     out = out.reshape(3, 8, 8, 128).transpose(1, 2, 0, 3)
     return out, ratio[0, 0]
 

time: 128 us -> 123 us (0.961)
  Pallas kernels: 122 us -> 119 us
  local copies, waits for them, and re-layouts: 2.88 us -> 1.54 us
    pallas_call x1, Pallas kernels: 122 us -> 119 us  [shards(): pl.pallas_call(kernel, out_shape=(jax.ShapeDtypeStruct((3, LOCAL, 128), F...]
    reshape x1 -> x0, local copies, waits for them, and re-layouts: 1.34 us -> none  [shards(): ids = block_list.reshape(1, ENTRIES)]
where the time goes in v2:
time: 123 us
  Pallas kernels  119 us (97%)
  between operations  3.11 us (3%)
  local copies, waits for them, and re-layouts  1.54 us (1%)
    pallas_call x1, Pallas kernels, shards(): pl.pallas_call(kernel, out_shape=(jax.ShapeDtypeStruct((3, LOCAL, 128), F...  119 us

profile of v2, /device:TPU:1, one launch (start us, length us, event | category | flops | bytes accessed | tf_op | source)
XLA Modules:
  0.0 123.3 jit_solution(13334373204309139448)
XLA Ops:
  1.3 118.7 %shard_map.68 = (f32[3,64,128]{2,1,0:T(8,128)}, f32[1,128]{1,0:T(1,128)}) custom-call(bf16[12,16,128,128]{3,2,1,0:T(8,128)(2,1)} %w_hbm.1, f32[12,48,128]{2,1,0:T(8,128)} %bitcast.10, s32[12,16]{1,0:T(8,128)} %ids_ref.1, f32[12,128]{1,0:T(8,128)} %obs_ref.1, s32[1,1]{1,0:T(1,128)S(6)} %copy.10.cnt_ref), custom_call_target="tpu_custom_call" | custom-call | tf_op jit(solution)/shard_map/pallas_call | solution.py:423
  119.9 1.5 %copy_bitcast_fusion = f32[8,8,3,128]{3,1,2,0:T(8,128)} fusion(f32[3,64,128]{2,1,0:T(8,128)} %get-tuple-element.4), kind=kLoop, calls=%fused_computation | loop fusion | bytes 196608 | tf_op jit(solution)/shard_map/transpose | solution.py:468

commit v3 on v2

--- a/solution.py
+++ b/solution.py
@@ -15,6 +15,7 @@
 BLOCKS = 16
 ENTRIES = TILES * BLOCKS
 DEVICES = 256
+CHIPS = 128
 N_SLAB = 8
 N_LAT = 32
 SLOTS = 2 * DEVICES
@@ -22,12 +23,31 @@
 ROW = 384
 ITERS = 3
 GROUPS = 8
-FAR = (4, 5, 3, 6)
-NEAR = (2, 7, 1, 0)
+
+Z_HALVES = ((4, 5, 3, 6), (2, 7, 1, 0))
+
+
+def ring(d, n):
+    return min(d, n - d)
+
+
+def block_order():
+    blocks = [(dx, dy, half) for dx in range(4) for dy in range(4) for half in range(2)]
+
+    def nearness(block):
+        dx, dy, half = block
+        far = ring(dx, 4) + ring(dy, 4) + (3, 1)[half]
+        return (-far, half, (dx * 3 + dy * 5) % 7, dx, dy)
+
+    return sorted(blocks, key=nearness)
+
+
+ORDER = block_order()
 GROUP = DEVICES // GROUPS
 EXCHANGES = 2 * ITERS
 HALOS = EXCHANGES - 1
 SUMS = EXCHANGES + 1
+SECOND_AT = 5
 LAM = 0.3
 EPS = 1e-6
 
@@ -56,8 +76,8 @@
 
 def kernel(
     w_hbm, ang_ref, ids_ref, obs_ref, cnt_ref, out_ref, ratio_ref,
-    W, WT, S, ST, STL, PICK, PICKT, RAY, PART, FETCH, LIVE,
-    X0, R0, X, R, V, FACE, HALO, AX, AY, AZ,
+    W, WT, S, ST, STL, PICK, PICKT, RAY, TRAV, PART, FETCH, LIVE,
+    X0, R0, X, R, V, FACE, HALO, AX, AY, AZ, ALL,
     wsem, xsend, xrecv, hsend, hrecv, s1, r1, s2, r2, entered,
 ):
     s, l = lax.axis_index("slab"), lax.axis_index("lat")
@@ -101,14 +121,17 @@
     dx, dz = ((lat_o & 3) - x) & 3, ((lat_o >> 2) - z) & 7
     dy, dc = ((slab_o >> 1) - y) & 3, ((slab_o & 1) - c) & 1
 
-    def far_first(d):
-        return jnp.where(d == 0, 3, jnp.where(d == 1, 2, jnp.where(d == 2, 0, 1)))
-
+    half = jnp.zeros_like(dz)
     place_z = jnp.zeros_like(dz)
-    for k in range(4):
-        place_z = jnp.where(dz == FAR[k], k, place_z)
-        place_z = jnp.where(dz == NEAR[k], 128 + k, place_z)
-    owner = place_z + 4 * ((far_first(dx) * 4 + far_first(dy)) * 2 + 1 - dc)
+    for h in range(2):
+        for k in range(4):
+            half = jnp.where(dz == Z_HALVES[h][k], h, half)
+            place_z = jnp.where(dz == Z_HALVES[h][k], k, place_z)
+    code = (dx * 4 + dy) * 2 + half
+    place_block = jnp.zeros_like(dz)
+    for n, (bx, by, bh) in enumerate(ORDER):
+        place_block = jnp.where(code == (bx * 4 + by) * 2 + bh, n, place_block)
+    owner = place_block * 8 + (1 - dc) * 4 + place_z
     owner_r, inner_r = owner.astype(F32), inner.astype(F32)
     square = (ENTRIES, ENTRIES)
     i0, i1 = iota(square, 0), iota(square, 1)
@@ -165,42 +188,79 @@
         total = jnp.sum(jnp.sum(AZ[n], axis=0), axis=1, keepdims=True)
         return jnp.sqrt(jnp.broadcast_to(total, (1, 128)) + EPS)
 
-    def buffers(e):
-        return (X0, R0) if e == 0 else (X.at[e - 1], R.at[e - 1])
-
-    def send_group(e, g, forward):
-        src, dst = buffers(e)
-        steps = FAR if g < GROUPS // 2 else NEAR
+    def sum_last(row):
+        n = SUMS - 1
+        AX[n, 0] = row
+        pair = pltpu.make_async_remote_copy(
+            AX.at[n, 0], AY.at[n, 0], s1.at[n], r1.at[n], device_id=(y * 2 + 1 - c, l), device_id_type=MESH
+        )
+        pair.start()
+        pair.wait()
+        row = row + AY[n, 0]
+        AX[n, 1] = row
+        ALL[CHIPS - 1] = row
+
+        def one(j, to_y, to_x, dz):
+            pltpu.make_async_remote_copy(
+                AX.at[n, 1], ALL.at[j], s2.at[n], r2.at[n],
+                device_id=(to_y * 2 + c, lax.rem(z + dz, 8) * 4 + to_x), device_id_type=MESH,
+            ).start()
 
         def offset(i):
             far = 3 - i
             return lax.rem(lax.div(far * (far + 1), 2), 4)
 
+        steps = Z_HALVES[0] + Z_HALVES[1]
+
+        @pl.loop(0, 15)
+        def _(q):
+            to_x = lax.rem(x + offset(lax.div(q, 4)), 4)
+            to_y = lax.rem(y + offset(lax.rem(q, 4)), 4)
+            for k in range(8):
+                one(q * 8 + k, to_y, to_x, steps[k])
+
+        for k in range(7):
+            one(120 + k, y, x, steps[k])
+        wait_bytes(ALL.at[pl.ds(0, CHIPS - 1)], r2.at[n])
+        total = jnp.sum(jnp.sum(ALL[...], axis=0), axis=1, keepdims=True)
+        return jnp.sqrt(jnp.broadcast_to(total, (1, 128)) + EPS)
+
+    def buffers(e):
+        return (X0, R0) if e == 0 else (X.at[e - 1], R.at[e - 1])
+
+    def send_group(e, g, forward):
+        src, dst = buffers(e)
+        blocks = ORDER[g * 4:(g + 1) * 4]
+
+        def of_block(b, values):
+            value = values[0]
+            for n in range(1, 4):
+                value = jnp.where(b == n, values[n], value)
+            return value
+
         def place(at, d, n):
             return lax.rem(at + n - d, n) if forward else lax.rem(at + d, n)
 
-        def one(q, k, to_x, to_slab):
-            j = (g // (GROUPS // 2)) * 128 + q * 4 + k
-            to_z = lax.rem(z + (8 - steps[k] if forward else steps[k]), 8)
+        def one(i, k, to_z, to_x, to_slab):
+            j = g * GROUP + i * 4 + k
             pltpu.make_async_remote_copy(
                 src.at[j], dst.at[j], xsend.at[e], xrecv.at[e, g],
                 device_id=(to_slab, to_z * 4 + to_x), device_id_type=MESH,
             ).start()
 
-        first = (g % (GROUPS // 2)) * (GROUP // 4)
-        last = first + GROUP // 4
-
-        @pl.loop(first, last - 1 if g == GROUPS - 1 else last)
-        def _(q):
-            to_x = place(x, offset(lax.div(q, 8)), 4)
-            to_y = place(y, offset(lax.rem(lax.div(q, 2), 4)), 4)
-            to_c = lax.rem(c + 1 - lax.rem(q, 2), 2)
+        @pl.loop(0, 7 if g == GROUPS - 1 else 8)
+        def _(i):
+            b = lax.div(i, 2)
+            to_x = place(x, of_block(b, [n[0] for n in blocks]), 4)
+            to_y = place(y, of_block(b, [n[1] for n in blocks]), 4)
+            to_c = lax.rem(c + 1 - lax.rem(i, 2), 2)
             for k in range(4):
-                one(q, k, to_x, to_y * 2 + to_c)
+                dz = of_block(b, [Z_HALVES[n[2]][k] for n in blocks])
+                one(i, k, place(z, dz, 8), to_x, to_y * 2 + to_c)
 
         if g == GROUPS - 1:
             for k in range(3):
-                one(31, k, x, s)
+                one(7, k, place(z, Z_HALVES[1][k], 8), x, s)
             pltpu.make_async_copy(src.at[DEVICES - 1], dst.at[DEVICES - 1], xrecv.at[e, g]).start()
 
     def receive_group(e, g):
@@ -267,7 +327,7 @@
         for p in range(3):
             PART[p, t * BLOCKS:(t + 1) * BLOCKS, :] = out[p * BLOCKS:(p + 1) * BLOCKS]
 
-    def send_adjoint(e, after_first):
+    def send_adjoint(e, beside):
         high = [PART[p].astype(BF16) for p in range(3)]
         low = [(PART[p] - high[p].astype(F32)).astype(BF16) for p in range(3)]
         high, low = jnp.concatenate(high, axis=1), jnp.concatenate(low, axis=1)
@@ -278,20 +338,24 @@
                 rows = jnp.concatenate([rows, wanted[g * 2 * GROUP:(g + 1) * 2 * GROUP]], axis=1)
             src = buffers(e)[0]
             src[pl.ds(g * GROUP, GROUP)] = rows.reshape(GROUP, 2, rows.shape[-1])
+            if g == 0:
+                beside()
             send_group(e, g, False)
-            if g == 0:
-                after_first()
-        sum_second(e)
-
-    def send_forward(e, model, after_first):
-        model = jnp.concatenate(model, axis=1).astype(BF16)
+            if g == SECOND_AT:
+                sum_second(e)
+
+    def send_forward(e, values):
+        model = jnp.concatenate(values, axis=1).astype(BF16)
         for g in range(GROUPS):
             rows = dot(PICK[pl.ds(g * 2 * GROUP, 2 * GROUP), :], model).astype(BF16)
             buffers(e)[0][pl.ds(g * GROUP, GROUP)] = rows.reshape(GROUP, 2, ROW)
+            if g == 0:
+                sum_first(e, total_row(sum(v * v for v in values)))
             send_group(e, g, True)
-            if g == 0:
-                after_first()
-        sum_second(e)
+            if g == 1:
+                send_halo(e - 1)
+            if g == SECOND_AT:
+                sum_second(e)
 
     def gather(e, table, groups, total=None):
         for g in groups:
@@ -344,13 +408,9 @@
         e = 2 * i + 1
         final = i == ITERS - 1
 
-        def beside_forward():
-            for p in range(3):
-                V[e - 1, p] = model_raw[p]
-            sum_first(e, total_row(sum(v * v for v in model_raw)))
-            send_halo(e - 1)
-
-        send_forward(e, model_raw, beside_forward)
+        for p in range(3):
+            V[e - 1, p] = model_raw[p]
+        send_forward(e, model_raw)
         smooth = laplace(e - 1)
         fetched = gather(e, S, most)
         v_norm = sum_third(e)
@@ -372,23 +432,21 @@
         known = v_norm * ray
         FETCH[...] = gather(e, S, rest, fetched).astype(BF16)
         for t in range(TILES):
-            row = forward_tile(t) * scale[t:t + 1] - known[t:t + 1]
-            RAY[t:t + 1, :] = row
-            if not final:
-                adjoint_tile(t, row)
-
-        def beside_adjoint():
-            ray_raw = RAY[...]
-            sum_first(e + 1, cell_sum + total_row(ray_raw * ray_raw))
+            TRAV[t:t + 1, :] = forward_tile(t)
+        ray_raw = TRAV[...] * scale - known
+        RAY[...] = ray_raw
+        for t in range(0 if final else TILES):
+            adjoint_tile(t, RAY[t:t + 1, :])
+
+        ray_sum = cell_sum + total_row(ray_raw * ray_raw)
 
         if not final:
-            send_adjoint(e + 1, beside_adjoint)
+            send_adjoint(e + 1, lambda: sum_first(e + 1, ray_sum))
             smooth = laplace(e)
             back = gather(e + 1, PICKT, most)
+            u_norm = sum_third(e + 1)
         else:
-            beside_adjoint()
-            sum_second(e + 1)
-        u_norm = sum_third(e + 1)
+            u_norm = sum_last(ray_sum)
         rho_now = jnp.sqrt(rho_bar * rho_bar + u_norm * u_norm)
         cos_term = rho_bar / rho_now
         sin_term = u_norm / rho_now
@@ -396,7 +454,7 @@
         phi_bar = sin_term * phi_bar
         result = [r + phi_now / rho_now * d for r, d in zip(result, direction)]
         if not final:
-            ray = RAY[...] / u_norm
+            ray = ray_raw / u_norm
             cell = [q / u_norm for q in cell_raw]
             known = [LAM * sm / u_norm - u_norm * m for sm, m in zip(smooth, model)]
             back = gather(e + 1, PICKT, rest, back)
@@ -411,9 +469,10 @@
     for h in range(HALOS):
         for side in range(4):
             wait_bytes(HALO.at[h, side], hsend.at[h, side])
-    for n in range(SUMS):
+    for n in range(SUMS - 1):
         wait_bytes(AY.at[n, pl.ds(0, 15)], s1.at[n])
         wait_bytes(AZ.at[n, pl.ds(0, 15)], s2.at[n])
+    wait_bytes(ALL.at[pl.ds(0, CHIPS - 1)], s2.at[SUMS - 1])
 
 
 def shards(weights, angles, block_list, observed, ray_count):
@@ -437,6 +496,7 @@
             pltpu.VMEM((SLOTS, LOCAL), BF16),
             pltpu.VMEM((GROUPS, LOCAL, 2 * GROUP), BF16),
             pltpu.VMEM((TILES, 128), F32),
+            pltpu.VMEM((TILES, 128), F32),
             pltpu.VMEM((3, ENTRIES, 128), F32),
             pltpu.VMEM((ENTRIES, ROW), BF16),
             pltpu.VMEM((TILES, 128), F32),
@@ -450,6 +510,7 @@
             pltpu.VMEM((SUMS, 2, 1, 128), F32),
             pltpu.VMEM((SUMS, 16, 1, 128), F32),
             pltpu.VMEM((SUMS, 16, 1, 128), F32),
+            pltpu.VMEM((CHIPS, 1, 128), F32),
             dma((TILES,)),
             dma((EXCHANGES,)),
             dma((EXCHANGES, GROUPS)),

time: 123 us -> 118 us (0.959)
  Pallas kernels: 119 us -> 113 us
    pallas_call x1, Pallas kernels: 119 us -> 113 us  [shards(): pl.pallas_call(kernel, out_shape=(jax.ShapeDtypeStruct((3, LOCAL, 128), F...]
where the time goes in v3:
time: 118 us
  Pallas kernels  113 us (96%)
  between operations  3.11 us (3%)
  local copies, waits for them, and re-layouts  1.54 us (1%)
    pallas_call x1, Pallas kernels, shards(): pl.pallas_call(kernel, out_shape=(jax.ShapeDtypeStruct((3, LOCAL, 128), F...  113 us

profile of v3, /device:TPU:1, one launch (start us, length us, event | category | flops | bytes accessed | tf_op | source)
XLA Modules:
  0.0 117.8 jit_solution(13945420001470384114)
XLA Ops:
  1.3 113.2 %shard_map.68 = (f32[3,64,128]{2,1,0:T(8,128)}, f32[1,128]{1,0:T(1,128)}) custom-call(bf16[12,16,128,128]{3,2,1,0:T(8,128)(2,1)} %w_hbm.1, f32[12,48,128]{2,1,0:T(8,128)} %bitcast.10, s32[12,16]{1,0:T(8,128)} %ids_ref.1, f32[12,128]{1,0:T(8,128)} %obs_ref.1, s32[1,1]{1,0:T(1,128)S(6)} %copy.10.cnt_ref), custom_call_target="tpu_custom_call" | custom-call | tf_op jit(solution)/shard_map/pallas_call | solution.py:482
  114.5 1.5 %copy_bitcast_fusion = f32[8,8,3,128]{3,1,2,0:T(8,128)} fusion(f32[3,64,128]{2,1,0:T(8,128)} %get-tuple-element.4), kind=kLoop, calls=%fused_computation | loop fusion | bytes 196608 | tf_op jit(solution)/shard_map/transpose | solution.py:529

commit v4 on v3

--- a/solution.py
+++ b/solution.py
@@ -75,10 +75,11 @@
 
 
 def kernel(
-    w_hbm, ang_ref, ids_ref, obs_ref, cnt_ref, out_ref, ratio_ref,
+    w_hbm, ang_hbm, ids_hbm, obs_hbm, cnt_hbm, out_hbm, ratio_hbm,
+    ang_ref, ids_ref, obs_ref, cnt_ref, out_ref, ratio_ref,
     W, WT, S, ST, STL, PICK, PICKT, RAY, TRAV, PART, FETCH, LIVE,
-    X0, R0, X, R, V, FACE, HALO, AX, AY, AZ, ALL,
-    wsem, xsend, xrecv, hsend, hrecv, s1, r1, s2, r2, entered,
+    X, R, V, FACE, HALO, AX, AY, AZ, ALL, ASK, ASKED,
+    wsem, xsend, xrecv, hsend, hrecv, s1, r1, s2, r2, q1, q2, isem, entered,
 ):
     s, l = lax.axis_index("slab"), lax.axis_index("lat")
     me = s * N_LAT + l
@@ -91,8 +92,12 @@
     def b_dev(j):
         return (lax.div(j, 4) * 2 + c, z * 4 + lax.rem(j, 4))
 
-    for t in range(TILES):
-        pltpu.make_async_copy(w_hbm.at[t], W.at[t], wsem.at[t]).start()
+    operands = [
+        pltpu.make_async_copy(src, dst, isem.at[n])
+        for n, (src, dst) in enumerate(
+            ((ids_hbm, ids_ref), (cnt_hbm, cnt_ref), (obs_hbm, obs_ref), (ang_hbm, ang_ref))
+        )
+    ]
 
     barrier = pltpu.get_barrier_semaphore()
 
@@ -100,6 +105,12 @@
     def _(j):
         pl.semaphore_signal(barrier, inc=1, device_id=a_dev(lax.rem(a_me + j, 16)), device_id_type=MESH)
         pl.semaphore_signal(barrier, inc=1, device_id=b_dev(lax.rem(b_me + j, 16)), device_id_type=MESH)
+
+    for copy in operands:
+        copy.start()
+    for t in range(TILES):
+        pltpu.make_async_copy(w_hbm.at[t], W.at[t], wsem.at[t]).start()
+    operands[0].wait()
 
     spread_k = jnp.where(
         (lax.broadcasted_iota(jnp.int32, (BLOCKS, ENTRIES), 1) & (BLOCKS - 1))
@@ -151,10 +162,81 @@
     stl = one_hot(iota((SLOTS, ENTRIES), 0) == spare_r)
     ST[...] = st
     STL[...] = stl
-    wanted = dot(st + stl, one_hot(iota((ENTRIES, 128), 1) == inner_c)).astype(BF16)
+
+    rank_r = slot_r - 2.0 * owner_r
+    a_r = ((lat_o >> 2) * 2 + (slab_o & 1)).astype(F32)
+    lane_r = 2.0 * ((slab_o >> 1) * 4 + (lat_o & 3)).astype(F32) + rank_r
+    lane_c = column(lane_r)
+    spare_c = column(jnp.where(alone, lane_r + 1.0, -1.0))
+    lanes = iota((ENTRIES, 128), 1)
+    asked = dot(
+        jnp.where(iota((16, ENTRIES), 0) == a_r, inner_r + 1.0, 0.0).astype(BF16),
+        one_hot(lanes == lane_c) + one_hot(lanes == spare_c),
+    )
+
+    def ask_first():
+        for i in range(16):
+            ASK[0, i] = asked[i:i + 1]
+        ASKED[0, a_me] = ASK[0, a_me]
+
+        @pl.loop(1, 16)
+        def _(j):
+            d = lax.rem(a_me + j, 16)
+            pltpu.make_async_remote_copy(
+                ASK.at[0, d], ASKED.at[0, a_me], q1.at[0], q1.at[1], device_id=a_dev(d), device_id_type=MESH
+            ).start()
+
+    def ask_second():
+        wait_bytes(ASKED.at[0, pl.ds(0, 15)], q1.at[1])
+        rows = jnp.concatenate([ASKED[0, i] for i in range(16)], axis=0).astype(BF16)
+        turned = None
+        for r in range(2):
+            mine = one_hot(iota((16, 128), 1) == 2.0 * iota((16, 128), 0) + float(r))
+            part = lax.dot_general(mine, rows, (((1,), (1,)), ((), ())), preferred_element_type=F32)
+            part = dot(part.astype(BF16), mine)
+            turned = part if turned is None else turned + part
+        for i in range(16):
+            ASK[1, i] = turned[i:i + 1]
+        ASKED[1, b_me] = ASK[1, b_me]
+
+        @pl.loop(1, 16)
+        def _(j):
+            d = lax.rem(b_me + j, 16)
+            pltpu.make_async_remote_copy(
+                ASK.at[1, d], ASKED.at[1, b_me], q2.at[0], q2.at[1], device_id=b_dev(d), device_id_type=MESH
+            ).start()
+
+    def ask_third():
+        slot = lax.broadcasted_iota(jnp.int32, (1, SLOTS), 1)
+        block, core, k = slot >> 4, (slot >> 3) & 1, (slot >> 1) & 3
+        from_x, from_y, half = jnp.zeros_like(slot), jnp.zeros_like(slot), jnp.zeros_like(slot)
+        for n, (bx, by, bh) in enumerate(ORDER):
+            here = block == n
+            from_x = jnp.where(here, (x - bx) & 3, from_x)
+            from_y = jnp.where(here, (y - by) & 3, from_y)
+            half = jnp.where(here, bh, half)
+        from_z = jnp.zeros_like(slot)
+        for h in range(2):
+            for n in range(4):
+                from_z = jnp.where(half * 4 + k == h * 4 + n, (z - Z_HALVES[h][n]) & 7, from_z)
+        from_c = (c + 1 - core) & 1
+        a_s = (from_z * 2 + from_c).astype(F32)
+        b_s = (from_y * 4 + from_x).astype(F32)
+        lane_s = 2.0 * a_s + (slot & 1).astype(F32)
+        lane_table = one_hot(iota((128, SLOTS), 0) == lane_s)
+        wait_bytes(ASKED.at[1, pl.ds(0, 15)], q2.at[1])
+        rows = jnp.concatenate([ASKED[1, i] for i in range(16)], axis=0).astype(BF16)
+        found = jnp.where(iota((16, SLOTS), 0) == b_s, dot(rows, lane_table), 0.0)
+        inner_s = jnp.sum(found, axis=0, keepdims=True) - 1.0
+        picked = jnp.where(iota((LOCAL, SLOTS), 0) == inner_s, 1.0, 0.0)
+        PICK[...] = picked.T.astype(BF16)
+        for g in range(GROUPS):
+            PICKT[g] = PICK[pl.ds(g * 2 * GROUP, 2 * GROUP), :].T
+
 
     at = iota((TILES, 128), 0) * 128.0 + iota((TILES, 128), 1)
-    LIVE[...] = jnp.where(at < cnt_ref[0, 0].astype(F32), 1.0, 0.0)
+    operands[1].wait()
+    LIVE[...] = jnp.where(at < cnt_ref[...].astype(F32), 1.0, 0.0)
 
     def total_row(values):
         return jnp.sum(values, axis=0, keepdims=True)
@@ -226,7 +308,7 @@
         return jnp.sqrt(jnp.broadcast_to(total, (1, 128)) + EPS)
 
     def buffers(e):
-        return (X0, R0) if e == 0 else (X.at[e - 1], R.at[e - 1])
+        return X.at[e], R.at[e]
 
     def send_group(e, g, forward):
         src, dst = buffers(e)
@@ -334,8 +416,6 @@
         for g in range(GROUPS):
             at = pl.ds(g * 2 * GROUP, 2 * GROUP)
             rows = (dot(ST[at, :], high) + dot(STL[at, :], low)).astype(BF16)
-            if e == 0:
-                rows = jnp.concatenate([rows, wanted[g * 2 * GROUP:(g + 1) * 2 * GROUP]], axis=1)
             src = buffers(e)[0]
             src[pl.ds(g * GROUP, GROUP)] = rows.reshape(GROUP, 2, rows.shape[-1])
             if g == 0:
@@ -366,6 +446,7 @@
     def by_parameter(total):
         return [total[:, p * 128:(p + 1) * 128] for p in range(3)]
 
+    operands[2].wait()
     ray = obs_ref[...] * LIVE[...]
     RAY[...] = ray
     pl.semaphore_wait(barrier, 30)
@@ -374,11 +455,14 @@
     def _(j):
         pl.semaphore_signal(entered, inc=1, device_id=b_dev(lax.rem(b_me + j, 16)), device_id_type=MESH)
 
+    operands[3].wait()
     for t in range(TILES):
         wait_bytes(W.at[t], wsem.at[t])
         adjoint_tile(t, RAY[t:t + 1, :])
     pl.semaphore_wait(entered, 15)
+    ask_first()
     send_adjoint(0, lambda: sum_first(0, total_row(ray * ray)))
+    ask_second()
 
     def turn(t, carry):
         for k in range(BLOCKS):
@@ -386,17 +470,12 @@
         return carry
 
     lax.fori_loop(0, TILES, turn, 0)
-    total = None
-    for g in range(GROUPS):
-        rows = receive_group(0, g)
-        pick = rows[:, ROW:ROW + LOCAL]
-        PICK[pl.ds(g * 2 * GROUP, 2 * GROUP), :] = pick
-        PICKT[g] = pick.T
-        part = dot(PICKT[g], rows[:, :ROW])
-        total = part if total is None else total + part
+    ask_third()
+    back = gather(0, PICKT, range(GROUPS - 1))
     first_norm = sum_third(0)
     ray = ray / first_norm
-    model_raw = [part / first_norm for part in by_parameter(total)]
+    back = gather(0, PICKT, range(GROUPS - 1, GROUPS), back)
+    model_raw = [part / first_norm for part in by_parameter(back)]
 
     cell = [jnp.zeros((LOCAL, 128), F32) for _ in range(3)]
     direction = model = smooth = None
@@ -463,6 +542,12 @@
     for p in range(3):
         out_ref[p] = result[p]
     ratio_ref[...] = phi_bar / first_norm
+    results = [
+        pltpu.make_async_copy(out_ref, out_hbm, isem.at[4]),
+        pltpu.make_async_copy(ratio_ref, ratio_hbm, isem.at[5]),
+    ]
+    for copy in results:
+        copy.start()
 
     for e in range(EXCHANGES):
         wait_bytes(buffers(e)[0].at[pl.ds(0, DEVICES - 1)], xsend.at[e])
@@ -473,11 +558,15 @@
         wait_bytes(AY.at[n, pl.ds(0, 15)], s1.at[n])
         wait_bytes(AZ.at[n, pl.ds(0, 15)], s2.at[n])
     wait_bytes(ALL.at[pl.ds(0, CHIPS - 1)], s2.at[SUMS - 1])
+    wait_bytes(ASKED.at[0, pl.ds(0, 15)], q1.at[0])
+    wait_bytes(ASKED.at[1, pl.ds(0, 15)], q2.at[0])
+    for copy in results:
+        copy.wait()
 
 
 def shards(weights, angles, block_list, observed, ray_count):
     ang = angles.transpose(0, 2, 1, 3).reshape(TILES, 3 * BLOCKS, 128)
-    vmem = pl.BlockSpec(memory_space=pltpu.VMEM)
+    anywhere = pl.BlockSpec(memory_space=pl.ANY)
     dma = pltpu.SemaphoreType.DMA
     out, ratio = pl.pallas_call(
         kernel,
@@ -485,9 +574,15 @@
             jax.ShapeDtypeStruct((3, LOCAL, 128), F32),
             jax.ShapeDtypeStruct((1, 128), F32),
         ),
-        in_specs=[pl.BlockSpec(memory_space=pl.ANY), vmem, vmem, vmem, pl.BlockSpec(memory_space=pltpu.SMEM)],
-        out_specs=(vmem, vmem),
+        in_specs=[anywhere] * 5,
+        out_specs=(anywhere, anywhere),
         scratch_shapes=[
+            pltpu.VMEM((TILES, 3 * BLOCKS, 128), F32),
+            pltpu.VMEM((TILES, BLOCKS), jnp.int32),
+            pltpu.VMEM((TILES, 128), F32),
+            pltpu.VMEM((1, 1), jnp.int32),
+            pltpu.VMEM((3, LOCAL, 128), F32),
+            pltpu.VMEM((1, 128), F32),
             pltpu.VMEM((TILES, BLOCKS, 128, 128), BF16),
             pltpu.VMEM((TILES, BLOCKS * 128, 128), BF16),
             pltpu.VMEM((GROUPS, ENTRIES, 2 * GROUP), BF16),
@@ -500,10 +595,8 @@
             pltpu.VMEM((3, ENTRIES, 128), F32),
             pltpu.VMEM((ENTRIES, ROW), BF16),
             pltpu.VMEM((TILES, 128), F32),
-            pltpu.VMEM((DEVICES, 2, ROW + 128), BF16),
-            pltpu.VMEM((DEVICES, 2, ROW + 128), BF16),
-            pltpu.VMEM((EXCHANGES - 1, DEVICES, 2, ROW), BF16),
-            pltpu.VMEM((EXCHANGES - 1, DEVICES, 2, ROW), BF16),
+            pltpu.VMEM((EXCHANGES, DEVICES, 2, ROW), BF16),
+            pltpu.VMEM((EXCHANGES, DEVICES, 2, ROW), BF16),
             pltpu.VMEM((HALOS, 3, LOCAL, 128), F32),
             pltpu.VMEM((HALOS, 2, 3, 8, 128), F32),
             pltpu.VMEM((HALOS, 4, 3, 8, 128), F32),
@@ -511,6 +604,8 @@
             pltpu.VMEM((SUMS, 16, 1, 128), F32),
             pltpu.VMEM((SUMS, 16, 1, 128), F32),
             pltpu.VMEM((CHIPS, 1, 128), F32),
+            pltpu.VMEM((2, 16, 1, 128), F32),
+            pltpu.VMEM((2, 16, 1, 128), F32),
             dma((TILES,)),
             dma((EXCHANGES,)),
             dma((EXCHANGES, GROUPS)),
@@ -520,6 +615,9 @@
             dma((SUMS,)),
             dma((SUMS,)),
             dma((SUMS,)),
+            dma((2,)),
+            dma((2,)),
+            dma((6,)),
             pltpu.SemaphoreType.REGULAR,
         ],
         compiler_params=pltpu.CompilerParams(

time: 118 us -> 115 us (0.975)
  Pallas kernels: 113 us -> 110 us
    pallas_call x1, Pallas kernels: 113 us -> 110 us  [shards(): pl.pallas_call(kernel, out_shape=(jax.ShapeDtypeStruct((3, LOCAL, 128), F...]
where the time goes in v4:
time: 115 us
  Pallas kernels  110 us (96%)
  between operations  3.11 us (3%)
  local copies, waits for them, and re-layouts  1.54 us (1%)
    pallas_call x1, Pallas kernels, shards(): pl.pallas_call(kernel, out_shape=(jax.ShapeDtypeStruct((3, LOCAL, 128), F...  110 us

profile of v4, /device:TPU:1, one launch (start us, length us, event | category | flops | bytes accessed | tf_op | source)
XLA Modules:
  0.0 114.9 jit_solution(10785108560866559281)
XLA Ops:
  1.3 110.2 %shard_map.68 = (f32[3,64,128]{2,1,0:T(8,128)}, f32[1,128]{1,0:T(1,128)}) custom-call(bf16[12,16,128,128]{3,2,1,0:T(8,128)(2,1)} %w_hbm.1, f32[12,48,128]{2,1,0:T(8,128)} %bitcast.10, s32[12,16]{1,0:T(8,128)} %ids_hbm.1, f32[12,128]{1,0:T(8,128)} %obs_hbm.1, s32[1,1]{1,0:T(1,128)S(6)} %copy.10.cnt_hbm), custom_call_target="tpu_custom_call" | custom-call | tf_op jit(solution)/shard_map/pallas_call | solution.py:571
  111.5 1.5 %copy_bitcast_fusion = f32[8,8,3,128]{3,1,2,0:T(8,128)} fusion(f32[3,64,128]{2,1,0:T(8,128)} %get-tuple-element.4), kind=kLoop, calls=%fused_computation | loop fusion | bytes 196608 | tf_op jit(solution)/shard_map/transpose | solution.py:627

commit v5 on v4

--- a/solution.py
+++ b/solution.py
@@ -36,7 +36,7 @@
 
     def nearness(block):
         dx, dy, half = block
-        far = ring(dx, 4) + ring(dy, 4) + (3, 1)[half]
+        far = ring(dx, 4) + ring(dy, 4) + (2, 1)[half]
         return (-far, half, (dx * 3 + dy * 5) % 7, dx, dy)
 
     return sorted(blocks, key=nearness)

time: 115 us -> 114 us (level)
  no operation moved by 1% of the time
where the time goes in v5:
time: 114 us
  Pallas kernels  109 us (96%)
  between operations  3.11 us (3%)
  local copies, waits for them, and re-layouts  1.54 us (1%)
    pallas_call x1, Pallas kernels, shards(): pl.pallas_call(kernel, out_shape=(jax.ShapeDtypeStruct((3, LOCAL, 128), F...  109 us

profile of v5, /device:TPU:1, one launch (start us, length us, event | category | flops | bytes accessed | tf_op | source)
XLA Modules:
  0.0 114.0 jit_solution(4450810207467290917)
XLA Ops:
  1.3 109.4 %shard_map.68 = (f32[3,64,128]{2,1,0:T(8,128)}, f32[1,128]{1,0:T(1,128)}) custom-call(bf16[12,16,128,128]{3,2,1,0:T(8,128)(2,1)} %w_hbm.1, f32[12,48,128]{2,1,0:T(8,128)} %bitcast.10, s32[12,16]{1,0:T(8,128)} %ids_hbm.1, f32[12,128]{1,0:T(8,128)} %obs_hbm.1, s32[1,1]{1,0:T(1,128)S(6)} %copy.10.cnt_hbm), custom_call_target="tpu_custom_call" | custom-call | tf_op jit(solution)/shard_map/pallas_call | solution.py:571
  110.6 1.5 %copy_bitcast_fusion = f32[8,8,3,128]{3,1,2,0:T(8,128)} fusion(f32[3,64,128]{2,1,0:T(8,128)} %get-tuple-element.4), kind=kLoop, calls=%fused_computation | loop fusion | bytes 196608 | tf_op jit(solution)/shard_map/transpose | solution.py:627
